TPU v7x, 32 devices: a whole 2x2x4 slice. The times are simulated.
32 devices in a mesh: groups: 2 (over y), expert: 4 (over z), dp: 2 (over x), head: 2 (over core).
Axes of the slice: x: 2, y: 2, z: 4, core: 2. Of those that a mesh axis runs over, the one named last changes fastest.
Arguments:
- queries: bfloat16 [32, 64, 128], P(('groups', 'expert', 'dp'), 'head'), parts along dimension 0, may hold values from -100 to 100
- new_key: bfloat16 [32, 4, 128], P(('groups', 'expert', 'dp'), 'head'), parts along dimension 0, may hold values from -4.5 to 4.5
- new_value: bfloat16 [32, 4, 128], P(('groups', 'expert', 'dp'), 'head'), parts along dimension 0, may hold values from -4.5 to 4.5
- key_cache: bfloat16 [32, 512, 4, 128], P(('groups', 'expert', 'dp'), None, 'head'), parts along dimension 0, may hold values from -4.5 to 4.5
- value_cache: bfloat16 [32, 512, 4, 128], P(('groups', 'expert', 'dp'), None, 'head'), parts along dimension 0, may hold values from -4.5 to 4.5
- lengths: int32 [32], P(('groups', 'expert', 'dp')), parts along dimension 0, may hold values from 2 to 512, as said below
- w_out: bfloat16 [8192, 4096], P('head', ('expert', 'dp')), may hold values from -0.0625 to 0.0625
- resid_cols: bfloat16 [32, 4096], P('groups', ('expert', 'dp')), parts along dimension 0, may hold values from -6 to 6
- norm_gain: float32 [4096], replicated, may hold values from 0.5 to 1.5
- router: bfloat16 [4096, 128], replicated, may hold values from -12 to 12
- routes: int32 [32, 8], P('groups'), parts along dimension 0, may hold values from 0 to 127, as said below
- capacity_slot: int32 [32], P('groups'), parts along dimension 0, may hold values from 0 to 3, as said below
- w_gate: bfloat16 [4, 4096, 1536], P('expert', 'head', 'dp'), may hold values from -0.09375 to 0.09375
- w_up: bfloat16 [4, 4096, 1536], P('expert', 'head', 'dp'), may hold values from -0.09375 to 0.09375
- w_down: bfloat16 [4, 1536, 4096], P('expert', 'dp', 'head'), may hold values from -0.15625 to 0.15625
Outputs:
- layer_out: bfloat16 [32, 4096], P(('groups', 'expert', 'dp'), 'head'), parts along dimension 0
There are 2 independent parts, one for each index of `groups`. A program takes and returns all parts, laid end to end along the dimension named above; an argument that names none is the same for every part. Nothing has to cross between parts.
Inputs may be any that keep to these rules, and one draw needn't show every extreme that they name: `routes`: each row names 8 different experts; exactly one of them is below 4, at a position that varies from row to row, and the others are 4 or more. capacity_slot[r] is row r's place among the rows whose expert below 4 is the same; these places run from 0 to that expert's row count minus 1. No expert below 4 has more than 4 rows, and one has exactly 4. `lengths`: some row has exactly 512 cached tokens.
All inputs are finite; a program needn't handle non-finite values.
Results may differ from a plain program's by a relative error of at most 0.0033.
The roundings to bfloat16 on the way count: a program that leaves them out, or rounds other values in their place, can miss the bound.
Values may be sent and summed in bfloat16 or wider, within the bound.
A program may use at most 64 MiB of HBM per device.

v0:
```python
import jax
import jax.numpy as jnp
from jax import lax
from jax.sharding import PartitionSpec as P


def rms_norm(hidden, gain):
    values = hidden.astype(jnp.float32)
    mean_square = jnp.mean(values * values, axis=-1, keepdims=True)
    return (values * lax.rsqrt(mean_square + 1e-06) * gain).astype(jnp.bfloat16)


def body(
    queries,
    new_key,
    new_value,
    key_cache,
    value_cache,
    lengths,
    w_out,
    resid_cols,
    norm_gain,
    router,
    routes,
    capacity_slot,
    w_gate,
    w_up,
    w_down,
):
    rows_dev, heads_dev, head_size = queries.shape
    cache_len = key_cache.shape[1]
    kv_dev = key_cache.shape[2]
    group_size = heads_dev // kv_dev
    score_scale = head_size ** (-0.5)
    query_block = queries.reshape(rows_dev, kv_dev, group_size, head_size)
    scores_cache = (
        jnp.einsum("rkgd,rlkd->rkgl", query_block, key_cache, preferred_element_type=jnp.float32)
        * score_scale
    )
    score_new = (
        jnp.einsum("rkgd,rkd->rkg", query_block, new_key, preferred_element_type=jnp.float32)
        * score_scale
    )
    valid_mask = jnp.arange(cache_len)[None, :] < lengths[:, None]
    scores_cache = jnp.where(valid_mask[:, None, None, :], scores_cache, -jnp.inf)
    highest = jnp.maximum(jnp.max(scores_cache, axis=-1), score_new)
    exp_cache = jnp.exp(scores_cache - highest[..., None])
    exp_new = jnp.exp(score_new - highest)
    denominator = jnp.sum(exp_cache, axis=-1) + exp_new
    probs_cache = (exp_cache / denominator[..., None]).astype(jnp.bfloat16)
    probs_new = (exp_new / denominator).astype(jnp.bfloat16)
    mixed = jnp.einsum(
        "rkgl,rlkd->rkgd", probs_cache, value_cache, preferred_element_type=jnp.float32
    )
    mixed = (
        mixed
        + probs_new.astype(jnp.float32)[..., None] * new_value.astype(jnp.float32)[:, :, None, :]
    )
    attn = mixed.astype(jnp.bfloat16).reshape(rows_dev, heads_dev * head_size)
    partial_proj = jnp.dot(
        lax.all_gather(attn, ("expert", "dp"), axis=0, tiled=True),
        w_out,
        preferred_element_type=jnp.float32,
    )
    attn_proj = lax.psum(partial_proj, "head")
    hidden_cols = (resid_cols.astype(jnp.float32) + attn_proj).astype(jnp.bfloat16)
    head_index = lax.axis_index("head")
    half_width = w_gate.shape[1]
    hidden_rows = lax.all_to_all(
        hidden_cols, ("expert", "dp"), split_axis=0, concat_axis=1, tiled=True
    )
    normed_own = rms_norm(hidden_rows, norm_gain)
    normed = lax.all_gather(normed_own, ("expert", "dp"), axis=0, tiled=True)
    hidden_own = lax.dynamic_slice_in_dim(hidden_rows, head_index * half_width, half_width, 1)
    all_rows = normed.shape[0]
    logits = jnp.dot(normed, router, preferred_element_type=jnp.float32)
    picked = routes[:, :, None] == jnp.arange(router.shape[1])[None, None, :]
    chosen_logits = jnp.sum(jnp.where(picked, logits[:, None, :], 0.0), axis=-1)
    gate_prob = jax.nn.softmax(chosen_logits, axis=-1)
    own = jnp.min(routes, axis=1)
    share = jnp.sum(jnp.where(routes == own[:, None], gate_prob, 0.0), axis=1)
    capacity = all_rows // 4
    expert_index = lax.axis_index("expert")
    is_mine = own == expert_index
    dispatch = (
        (jnp.arange(capacity)[:, None] == capacity_slot[None, :]) & is_mine[None, :]
    ).astype(jnp.bfloat16)
    buffer = jnp.dot(dispatch, normed, preferred_element_type=jnp.float32).astype(jnp.bfloat16)
    mine_half = lax.dynamic_slice_in_dim(buffer, head_index * half_width, half_width, 1)
    gate_local = w_gate[0]
    up_local = w_up[0]
    down_local = w_down[0]
    gate_part = jnp.dot(mine_half, gate_local, preferred_element_type=jnp.float32)
    up_part = jnp.dot(mine_half, up_local, preferred_element_type=jnp.float32)
    expert_gate, expert_up = lax.psum((gate_part, up_part), "head")
    activated = (jax.nn.silu(expert_gate) * expert_up).astype(jnp.bfloat16)
    expert_out = jnp.dot(activated, down_local, preferred_element_type=jnp.float32)
    row_share = jnp.where(is_mine, share, 0.0)
    routed = lax.psum_scatter(
        jnp.take(expert_out, capacity_slot, axis=0) * row_share[:, None],
        ("expert", "dp"),
        scatter_dimension=0,
        tiled=True,
    )
    return (hidden_own.astype(jnp.float32) + routed).astype(jnp.bfloat16)


def solution(mesh):
    in_specs = (
        P(("groups", "expert", "dp"), "head", None),
        P(("groups", "expert", "dp"), "head", None),
        P(("groups", "expert", "dp"), "head", None),
        P(("groups", "expert", "dp"), None, "head", None),
        P(("groups", "expert", "dp"), None, "head", None),
        P(("groups", "expert", "dp")),
        P("head", ("expert", "dp")),
        P("groups", ("expert", "dp")),
        P(),
        P(),
        P("groups", None),
        P("groups"),
        P("expert", "head", "dp"),
        P("expert", "head", "dp"),
        P("expert", "dp", "head"),
    )
    out_specs = P(("groups", "expert", "dp"), "head")
    return jax.shard_map(body, mesh=mesh, in_specs=in_specs, out_specs=out_specs, check_vma=False)
```

profile of v0, /device:TPU:0, one launch (start us, length us, event | category | flops | bytes accessed | tf_op | source)
XLA Modules:
  0.0 180.6 jit_solution(7090516381002476231)
XLA Ops:
  6.5 0.0 copy-start
  6.5 0.9 iota_compare_fusion.1
  7.4 0.9 fusion.20
  8.3 1.4 fusion.32
  9.7 0.0 copy-start.4
  9.7 0.0 copy-start.5
  9.8 0.0 copy-start.3
  9.8 0.2 fusion.10
  9.9 0.0 copy-start.2
  10.0 0.7 convert_element_type.47
  10.7 1.3 fusion.7
  12.0 32.3 %all-gather = bf16[8,2,4096]{2,1,0:T(2,128)(2,1)S(1)} all-gather(bf16[1,2,4096]{2,1,0:T(2,128)(2,1)S(1)} %reshape.70), channel_id=1, replica_groups=mesh['groups'=2,'expert'=4,'dp'=2,'head'=2] {'expert','dp'}, dimensions={0}, use_global_device_ids=true | all-gather | bytes 147456 | tf_op jit(solution)/shard_map/all_gather | solution.py:61
  44.3 0.1 reshape.71
  44.3 2.8 %fusion.33 = f32[16,512]{1,0:T(8,128)S(1)} fusion(bf16[16,4096]{1,0:T(8,128)(2,1)S(1)} %reshape.71, bf16[4096,512]{1,0:T(8,128)(2,1)} %param.21), kind=kOutput, calls=%fused_computation.58 | convolution fusion | flops 67108864 | bytes 4358144 | tf_op jit(solution)/shard_map/dot_general | solution.py:60
  47.2 3.4 %psum.21 = f32[16,512]{1,0:T(8,128)S(1)} all-reduce(f32[16,512]{1,0:T(8,128)S(1)} %fusion.33), channel_id=1, replica_groups=mesh['groups'=2,'expert'=4,'dp'=2,'head'=2] {'head'}, use_global_device_ids=true, to_apply=%region_2.3 | all-reduce | flops 8192 | bytes 65536 | tf_op jit(solution)/shard_map/psum | solution.py:65
  50.6 0.0 copy-done.4
  50.6 0.6 all_to_all.14
  51.2 5.5 %all-to-all-start = ((bf16[8,2,512]{2,1,0:T(2,128)(2,1)}), bf16[8,2,512]{2,1,0:T(2,128)(2,1)S(1)}, u32[]{:S(2)}, u32[]{:S(2)}) async-start(bf16[8,2,512]{2,1,0:T(2,128)(2,1)} %all_to_all.14), calls=%async_computation | async-start | bytes 32768 | tf_op jit(solution)/shard_map/all_to_all | solution.py:69
  56.7 0.0 all-reduce.4.cloned.1.call-start
  56.7 0.0 copy-done.5
  56.8 0.0 copy-done.3
  56.8 0.1 copy.24
  56.9 6.4 %all-to-all-done = bf16[8,2,512]{2,1,0:T(2,128)(2,1)S(1)} async-done(((bf16[8,2,512]{2,1,0:T(2,128)(2,1)}), bf16[8,2,512]{2,1,0:T(2,128)(2,1)S(1)}, u32[]{:S(2)}, u32[]{:S(2)}) %all-to-all-start) | async-done | bytes 16416 | tf_op jit(solution)/shard_map/all_to_all | solution.py:69
  63.2 0.1 multiply_reduce_fusion
  63.4 0.0 copy-done.2
  63.4 0.1 fusion.14
  63.5 30.5 %all-gather.1 = bf16[8,2,4096]{2,1,0:T(2,128)(2,1)S(1)} all-gather(bf16[1,2,4096]{2,1,0:T(2,128)(2,1)S(1)} %fusion.14), channel_id=1, replica_groups=mesh['groups'=2,'expert'=4,'dp'=2,'head'=2] {'expert','dp'}, dimensions={0}, use_global_device_ids=true | all-gather | bytes 147456 | tf_op jit(solution)/shard_map/all_gather | solution.py:73
  94.0 0.1 reshape.73
  94.1 1.5 fusion.34
  95.6 0.2 select_reduce_fusion
  95.7 0.1 reduce_max.19
  95.9 0.0 copy-start.1
  95.9 0.2 fusion.17
  96.0 0.2 select_reduce_fusion.1
  96.2 0.2 fusion.23
  96.4 2.7 %fusion.4 = f32[4,768]{1,0:T(4,128)S(1)} fusion(bf16[1,2048,768]{2,1,0:T(8,128)(2,1)} %param.27, bf16[4,4096]{1,0:T(4,128)(2,1)S(1)} %fusion.23, s32[]{:T(128)S(6)} %select_n.34), kind=kOutput, calls=%fused_computation.5 | convolution fusion | flops 12582912 | bytes 3174404 | tf_op jit(solution)/shard_map/dot_general | solution.py:93
  99.1 0.0 copy-done.1
  99.1 0.5 fusion.2
  99.6 0.0 copy-start.6
  99.6 3.5 %all-reduce.1 = (f32[4,768]{1,0:T(4,128)S(1)}, f32[4,768]{1,0:T(4,128)S(1)}) all-reduce(f32[4,768]{1,0:T(4,128)S(1)} %fusion.2, f32[4,768]{1,0:T(4,128)S(1)} %fusion.4), channel_id=1, replica_groups=mesh['groups'=2,'expert'=4,'dp'=2,'head'=2] {'head'}, use_global_device_ids=true, to_apply=%region_6.7 | all-reduce | flops 6144 | bytes 49152 | tf_op jit(solution)/shard_map/psum | solution.py:95
  103.2 0.0 copy-done
  103.2 0.5 fusion
  103.7 0.6 gather_fusion
  104.3 0.7 select_multiply_fusion
  105.0 0.0 all-reduce.4.cloned.1.call-update
  105.0 0.0 copy-done.6
  105.1 0.6 dynamic-slice
  106.3 66.0 %all-reduce.4.cloned.1.call-done = f32[16,2048]{1,0:T(8,128)} async-done(((f32[16,2048]{1,0:T(8,128)}), f32[16,2048]{1,0:T(8,128)}) %all-reduce.4.cloned.1.call-update) | async-done | bytes 131088
  172.3 1.5 fusion.13
  (10 shorter events, 0.1 us)
Async XLA Ops:
  6.5 96.6 %copy-start = (bf16[1,768,2048]{2,1,0:T(8,128)(2,1)S(1)}, bf16[1,768,2048]{2,1,0:T(8,128)(2,1)}, u32[]{:S(2)}) copy-start(bf16[1,768,2048]{2,1,0:T(8,128)(2,1)} %param.29) | copy-start | bytes 9437188
  9.7 40.9 %copy-start.4 = (bf16[16,512]{1,0:T(8,128)(2,1)S(1)}, bf16[16,512]{1,0:T(8,128)(2,1)}, u32[]{:S(2)}) copy-start(bf16[16,512]{1,0:T(8,128)(2,1)} %param.22) | copy-start | bytes 49156
  9.7 47.0 %copy-start.5 = (s32[16]{0:T(128)S(1)}, s32[16]{0:T(128)}, u32[]{:S(2)}) copy-start(s32[16]{0:T(128)} %param.26) | copy-start | bytes 196
  9.8 47.0 %copy-start.3 = (s32[16,8]{0,1:T(8,128)S(1)}, s32[16,8]{0,1:T(8,128)}, u32[]{:S(2)}) copy-start(s32[16,8]{0,1:T(8,128)} %param.25) | copy-start | bytes 1540
  9.9 53.5 %copy-start.2 = (f32[4096]{0:T(1024)S(1)}, f32[4096]{0:T(1024)}, u32[]{:S(2)}) copy-start(f32[4096]{0:T(1024)} %param.23) | copy-start | bytes 49156
  51.2 12.0 %all-to-all-start = ((bf16[8,2,512]{2,1,0:T(2,128)(2,1)}), bf16[8,2,512]{2,1,0:T(2,128)(2,1)S(1)}, u32[]{:S(2)}, u32[]{:S(2)}) async-start(bf16[8,2,512]{2,1,0:T(2,128)(2,1)} %all_to_all.14), calls=%async_computation | async-start | bytes 32768 | tf_op jit(solution)/shard_map/all_to_all | solution.py:69
  56.7 115.6 %all-reduce.4.cloned.1.call-start = ((), (), s32[]{:S(2)}) async-start(), calls=%async_computation.1 | async-start | bytes 262144
  95.9 3.2 %copy-start.1 = (bf16[1,2048,768]{2,1,0:T(8,128)(2,1)S(1)}, bf16[1,2048,768]{2,1,0:T(8,128)(2,1)}, u32[]{:S(2)}) copy-start(bf16[1,2048,768]{2,1,0:T(8,128)(2,1)} %param.28) | copy-start | bytes 9437188
  99.6 5.4 %copy-start.6 = (u32[32]{0:T(128)S(1)}, u32[32]{0:T(128)}, u32[]{:S(2)}) copy-start(u32[32]{0:T(128)} %constant.59) | copy-start | bytes 388
Sparse Core Ops, SparseCore 0:
  105.2 67.0 all-reduce.3
where the time goes:
time: 181 us
  waiting for transfers between devices  72.4 us (40%)
  blocking collectives  69.8 us (39%)
  between operations  14.2 us (8%)
  matrix products  11.8 us (7%)
  starting transfers between devices  5.5 us (3%)
  other arithmetic  4.9 us (3%)
  local copies, waits for them, and re-layouts  2.01 us (1%)
    unnamed x2, waiting for transfers between devices  66 us
    all_gather x1, blocking collectives, body(): lax.all_gather(attn, ('expert', 'dp'), axis=0, tiled=True)  32.3 us
    all_gather x1, blocking collectives, body(): normed = lax.all_gather(normed_own, ('expert', 'dp'), axis=0, tiled=True)  30.5 us
    all_to_all x1, waiting for transfers between devices, body(): lax.all_to_all(hidden_cols, ('expert', 'dp'), split_axis=0, concat_axis=1...  6.37 us
    all_to_all x1, starting transfers between devices, body(): lax.all_to_all(hidden_cols, ('expert', 'dp'), split_axis=0, concat_axis=1...  5.46 us
  transfers between devices with their start and end apart: 2, of which 2 were waited for; matrix products, arithmetic and copies ran while one was open for 0% of the time, Pallas kernels for 0%

commit v1 on v0

--- a/solution.py
+++ b/solution.py
@@ -1,6 +1,10 @@
+import functools
+
 import jax
 import jax.numpy as jnp
 from jax import lax
+from jax.experimental import pallas as pl
+from jax.experimental.pallas import tpu as pltpu
 from jax.sharding import PartitionSpec as P
 
 
@@ -10,7 +14,7 @@
     return (values * lax.rsqrt(mean_square + 1e-06) * gain).astype(jnp.bfloat16)
 
 
-def body(
+def plain_body(
     queries,
     new_key,
     new_value,
@@ -105,6 +109,468 @@
     return (hidden_own.astype(jnp.float32) + routed).astype(jnp.bfloat16)
 
 
+MESH = pl.DeviceIdType.MESH
+F32, BF16 = jnp.float32, jnp.bfloat16
+
+
+def step_kernel(
+    experts_axis,
+    dp_axis,
+    lengths,
+    queries,
+    new_key,
+    new_value,
+    keys,
+    values,
+    w_out,
+    resid,
+    gain,
+    router,
+    routes,
+    w_gate,
+    w_up,
+    w_down,
+    out,
+    q_v,
+    k_v,
+    v_v,
+    wo_v,
+    res_v,
+    gain_v,
+    rt_v,
+    routes_v,
+    wg_v,
+    wu_v,
+    wd_v,
+    attn_all,
+    attn_f32,
+    attn_mat,
+    proj_mine,
+    proj_other,
+    hid_send,
+    hid_all,
+    sq_all,
+    gate_mine,
+    gate_other,
+    up_mine,
+    up_other,
+    logit_mine,
+    logit_other,
+    y_send,
+    y_recv,
+    load_sem,
+    attn_ssem,
+    attn_rsem,
+    hid_ssem,
+    hid_rsem,
+    sq_ssem,
+    sq_rsem,
+    pair_ssem,
+    pair_rsem,
+    y_ssem,
+    y_rsem,
+):
+    blocks = experts_axis * dp_axis
+    half_blocks = blocks // 2
+    expert, dp, head = lax.axis_index("expert"), lax.axis_index("dp"), lax.axis_index("head")
+    me = expert * dp_axis + dp
+    rows_dev, heads_dev, head_size = queries.shape
+    rows = rows_dev * blocks
+    half_width = w_gate.shape[0]
+    cols = w_out.shape[1]
+    kv_dev = new_key.shape[1]
+    group_size = heads_dev // kv_dev
+
+    def device(block, head_index):
+        return {
+            "expert": lax.div(block, dp_axis),
+            "dp": lax.rem(block, dp_axis),
+            "head": head_index,
+        }
+
+    def peer(k):
+        return lax.rem(me + k, blocks)
+
+    barrier = pltpu.get_barrier_semaphore()
+    for k in range(blocks):
+        if k:
+            pl.semaphore_signal(barrier, 1, device_id=device(peer(k), head), device_id_type=MESH)
+        pl.semaphore_signal(barrier, 1, device_id=device(peer(k), 1 - head), device_id_type=MESH)
+
+    half_start = pl.multiple_of(head * half_width, half_width)
+    loads = [
+        pltpu.make_async_copy(src, dst, load_sem.at[i])
+        for i, (src, dst) in enumerate(
+            (
+                (queries, q_v),
+                (keys, k_v),
+                (values, v_v),
+                (w_out, wo_v),
+                (resid, res_v),
+                (gain.at[:, pl.ds(half_start, half_width)], gain_v),
+                (routes, routes_v),
+                (router.at[pl.ds(half_start, half_width), :], rt_v),
+                (w_gate, wg_v),
+                (w_up, wu_v),
+                (w_down, wd_v),
+            )
+        )
+    ]
+    for load in loads:
+        load.start()
+    (ld_q, ld_k, ld_v, ld_wo, ld_res, ld_gain, ld_routes, ld_rt, ld_wg, ld_wu, ld_wd) = loads
+
+    cached = keys.shape[1]
+    scale = head_size ** (-0.5)
+    column = lax.broadcasted_iota(jnp.int32, (heads_dev, cached), 1)
+    head_of = lax.broadcasted_iota(jnp.int32, (heads_dev, cached), 0)
+    position = lax.div(column, kv_dev)
+    same_kv = lax.rem(column, kv_dev) == lax.div(head_of, group_size)
+    kv_of = lax.div(lax.broadcasted_iota(jnp.int32, (heads_dev, head_size), 0), group_size)
+    ld_q.wait()
+    ld_k.wait()
+    ld_v.wait()
+    for r in range(rows_dev):
+        q = q_v[r]
+        scores = (
+            lax.dot_general(q, k_v[r], (((1,), (1,)), ((), ())), preferred_element_type=F32)
+            * scale
+        )
+        fresh_key = jnp.zeros((heads_dev, head_size), F32)
+        fresh_value = jnp.zeros((heads_dev, head_size), F32)
+        for k in range(kv_dev):
+            fresh_key = jnp.where(kv_of == k, new_key[r, k : k + 1, :].astype(F32), fresh_key)
+            fresh_value = jnp.where(kv_of == k, new_value[r, k : k + 1, :].astype(F32), fresh_value)
+        score_new = jnp.sum(q.astype(F32) * fresh_key, axis=-1, keepdims=True) * scale
+        scores = jnp.where(same_kv & (position < lengths[r]), scores, -jnp.inf)
+        highest = jnp.maximum(jnp.max(scores, axis=-1, keepdims=True), score_new)
+        exp_cache = jnp.exp(scores - highest)
+        exp_new = jnp.exp(score_new - highest)
+        inverse = 1.0 / (jnp.sum(exp_cache, axis=-1, keepdims=True) + exp_new)
+        probs = (exp_cache * inverse).astype(BF16)
+        probs_new = (exp_new * inverse).astype(BF16).astype(F32)
+        mixed = jnp.dot(probs, v_v[r], preferred_element_type=F32) + probs_new * fresh_value
+        attn_all[me, r * heads_dev : (r + 1) * heads_dev, :] = mixed.astype(BF16)
+
+    pl.semaphore_wait(barrier, 2 * blocks - 1)
+
+    def exchange(buffer, ssem, rsem, k):
+        to = peer(k)
+        return pltpu.make_async_remote_copy(
+            src_ref=buffer.at[me],
+            dst_ref=buffer.at[me],
+            send_sem=ssem.at[to],
+            recv_sem=rsem.at[me],
+            device_id=device(to, head),
+            device_id_type=MESH,
+        )
+
+    def arrival(src, dst, ssem, rsem, block):
+        return pltpu.make_async_remote_copy(
+            src_ref=src,
+            dst_ref=dst,
+            send_sem=ssem.at[block],
+            recv_sem=rsem.at[block],
+            device_id=device(block, head),
+            device_id_type=MESH,
+        )
+
+    def to_sibling(src, dst, i):
+        return pltpu.make_async_remote_copy(
+            src_ref=src,
+            dst_ref=dst,
+            send_sem=pair_ssem.at[i],
+            recv_sem=pair_rsem.at[i],
+            device_id=device(me, 1 - head),
+            device_id_type=MESH,
+        )
+
+    sends = [exchange(attn_all, attn_ssem, attn_rsem, k) for k in range(1, blocks)]
+    for copy in sends:
+        copy.start()
+    block_rows = rows_dev * heads_dev
+
+    def widen(block):
+        start = pl.multiple_of(block * block_rows, block_rows)
+        attn_f32[pl.ds(start, block_rows), :] = attn_all[block].astype(F32)
+
+    widen(me)
+
+    ld_routes.wait()
+    picks = routes_v[...]
+    expert_ids = lax.broadcasted_iota(jnp.int32, (rows, router.shape[1]), 1)
+    picked = expert_ids == picks[:, 0:1]
+    for k in range(1, picks.shape[1]):
+        picked = picked | (expert_ids == picks[:, k : k + 1])
+    own = jnp.min(picks, axis=1, keepdims=True)
+    is_mine = own == expert
+
+    for k in range(1, blocks):
+        block = peer(blocks - k)
+        arrival(attn_all.at[block], attn_all.at[block], attn_ssem, attn_rsem, block).wait_recv()
+        widen(block)
+    for h in range(heads_dev):
+        attn_mat[:, h * head_size : (h + 1) * head_size] = attn_f32[
+            pl.ds(h, rows, stride=heads_dev), :
+        ].astype(BF16)
+
+    ld_wo.wait()
+    proj_mine[...] = jnp.dot(attn_mat[...], wo_v[...], preferred_element_type=F32)
+    proj_copy = to_sibling(proj_mine, proj_other, 0)
+    proj_copy.start()
+    ld_res.wait()
+    ld_gain.wait()
+    proj_copy.wait_recv()
+    hidden = (res_v[...].astype(F32) + (proj_mine[...] + proj_other[...])).astype(BF16)
+    hid_send[...] = hidden
+    squares = hidden.astype(F32)
+    squares = jnp.sum(squares * squares, axis=-1, keepdims=True)
+    row_is_lane = lax.broadcasted_iota(jnp.int32, (rows, 128), 0) == lax.broadcasted_iota(
+        jnp.int32, (rows, 128), 1
+    )
+    half_of = lax.div(me, half_blocks)
+    slot = lax.rem(me, half_blocks)
+    stays = head == half_of
+    target_dp = lax.rem(dp + jnp.where(stays, 0, 1), dp_axis)
+
+    def hid_copy(k):
+        to = lax.rem(expert + k, experts_axis)
+        return pltpu.make_async_remote_copy(
+            src_ref=hid_send,
+            dst_ref=hid_all.at[slot],
+            send_sem=hid_ssem.at[k],
+            recv_sem=hid_rsem.at[slot],
+            device_id={"expert": to, "dp": target_dp, "head": half_of},
+            device_id_type=MESH,
+        )
+
+    for k in range(1, experts_axis):
+        hid_copy(k).start()
+
+    @pl.when(jnp.logical_not(stays))
+    def _():
+        hid_copy(0).start()
+
+    @pl.when(stays)
+    def _():
+        hid_all[slot] = hidden
+
+    sq_all[me] = jnp.sum(jnp.where(row_is_lane, squares, 0.0), axis=0, keepdims=True)
+    sq_sends = [exchange(sq_all, sq_ssem, sq_rsem, k) for k in range(1, blocks)]
+    for copy in sq_sends:
+        copy.start()
+    total = sq_all[me]
+    for k in range(1, blocks):
+        block = peer(blocks - k)
+        arrival(sq_all.at[block], sq_all.at[block], sq_ssem, sq_rsem, block).wait_recv()
+        total = total + sq_all[block]
+    total = jnp.sum(jnp.where(row_is_lane, total, 0.0), axis=1, keepdims=True)
+    inverse_rms = lax.rsqrt(total / (2 * half_width) + 1e-06)
+    for i in range(half_blocks):
+
+        @pl.when(jnp.logical_not(stays & (slot == i)))
+        def _():
+            pltpu.make_async_remote_copy(
+                src_ref=hid_send,
+                dst_ref=hid_all.at[i],
+                send_sem=hid_ssem.at[0],
+                recv_sem=hid_rsem.at[i],
+                device_id=device(me, 1 - head),
+                device_id_type=MESH,
+            ).wait_recv()
+
+    row_index = lax.broadcasted_iota(jnp.int32, (rows, 1), 0)
+    is_own_row = lax.div(row_index, rows_dev) == me
+    kept, pieces = [], []
+    for i in range(half_blocks):
+        values_f32 = hid_all[i].astype(F32)
+        kept.append(jnp.where(is_own_row, values_f32, 0.0))
+        pieces.append(
+            (values_f32 * inverse_rms * gain_v[:, i * cols : (i + 1) * cols]).astype(BF16)
+        )
+    normed = jnp.concatenate(pieces, axis=1)
+
+    ld_wg.wait()
+    gate_mine[...] = jnp.dot(normed, wg_v[...], preferred_element_type=F32)
+    gate_copy = to_sibling(gate_mine, gate_other, 1)
+    gate_copy.start()
+    ld_rt.wait()
+    logit_mine[...] = jnp.dot(normed, rt_v[...], preferred_element_type=F32)
+    logit_copy = to_sibling(logit_mine, logit_other, 2)
+    logit_copy.start()
+    ld_wu.wait()
+    up_mine[...] = jnp.dot(normed, wu_v[...], preferred_element_type=F32)
+    up_copy = to_sibling(up_mine, up_other, 3)
+    up_copy.start()
+
+    logit_copy.wait_recv()
+    logits = jnp.where(picked, logit_mine[...] + logit_other[...], -jnp.inf)
+    weights = jnp.exp(logits - jnp.max(logits, axis=1, keepdims=True))
+    share = jnp.sum(jnp.where(expert_ids == own, weights, 0.0), axis=1, keepdims=True) / jnp.sum(
+        weights, axis=1, keepdims=True
+    )
+    row_share = jnp.where(is_mine, share, 0.0)
+    gate_copy.wait_recv()
+    gate = gate_mine[...] + gate_other[...]
+    gate = gate / (1.0 + jnp.exp(-gate))
+    ld_wd.wait()
+    up_copy.wait_recv()
+    activated = (gate * (up_mine[...] + up_other[...])).astype(BF16)
+    routed = jnp.dot(activated, wd_v[...], preferred_element_type=F32) * row_share
+    routed = routed + jnp.concatenate(kept, axis=1)
+    for block in range(blocks):
+        y_send[block] = routed[block * rows_dev : (block + 1) * rows_dev, :]
+
+    y_sends = []
+    for k in range(1, blocks):
+        to = peer(k)
+        y_sends.append(
+            pltpu.make_async_remote_copy(
+                src_ref=y_send.at[to],
+                dst_ref=y_recv.at[me],
+                send_sem=y_ssem.at[to],
+                recv_sem=y_rsem.at[me],
+                device_id=device(to, head),
+                device_id_type=MESH,
+            )
+        )
+    for copy in y_sends:
+        copy.start()
+    result = y_send[me]
+    for k in range(1, blocks):
+        block = peer(blocks - k)
+        arrival(y_send.at[block], y_recv.at[block], y_ssem, y_rsem, block).wait_recv()
+        result = result + y_recv[block]
+    out[...] = result
+
+    for copy in sends + sq_sends + y_sends + [proj_copy, gate_copy, logit_copy, up_copy]:
+        copy.wait_send()
+    for k in range(1, experts_axis):
+        hid_copy(k).wait_send()
+
+    @pl.when(jnp.logical_not(stays))
+    def _():
+        hid_copy(0).wait_send()
+
+
+def body(
+    experts_axis,
+    dp_axis,
+    queries,
+    new_key,
+    new_value,
+    key_cache,
+    value_cache,
+    lengths,
+    w_out,
+    resid_cols,
+    norm_gain,
+    router,
+    routes,
+    capacity_slot,
+    w_gate,
+    w_up,
+    w_down,
+):
+    blocks = experts_axis * dp_axis
+    rows_dev, heads_dev, head_size = queries.shape
+    cache_len, kv_dev = key_cache.shape[1:3]
+    rows = rows_dev * blocks
+    cols = w_out.shape[1]
+    half_width, ff_dev = w_gate.shape[1:]
+    names = router.shape[1]
+    if cols % 128 or ff_dev % 128 or rows > 64 or rows % 16 or blocks % 2 or dp_axis != 2:
+        return plain_body(
+            queries,
+            new_key,
+            new_value,
+            key_cache,
+            value_cache,
+            lengths,
+            w_out,
+            resid_cols,
+            norm_gain,
+            router,
+            routes,
+            capacity_slot,
+            w_gate,
+            w_up,
+            w_down,
+        )
+    half_blocks = blocks // 2
+    dma = pltpu.SemaphoreType.DMA
+    any_spec = pl.BlockSpec(memory_space=pl.ANY)
+    vmem_spec = pl.BlockSpec(memory_space=pltpu.VMEM)
+    cached = cache_len * kv_dev
+    scratch = [
+        pltpu.VMEM((rows_dev, heads_dev, head_size), BF16),
+        pltpu.VMEM((rows_dev, cached, head_size), BF16),
+        pltpu.VMEM((rows_dev, cached, head_size), BF16),
+        pltpu.VMEM(w_out.shape, BF16),
+        pltpu.VMEM(resid_cols.shape, BF16),
+        pltpu.VMEM((1, half_width), F32),
+        pltpu.VMEM((half_width, names), BF16),
+        pltpu.VMEM(routes.shape, jnp.int32),
+        pltpu.VMEM((half_width, ff_dev), BF16),
+        pltpu.VMEM((half_width, ff_dev), BF16),
+        pltpu.VMEM((ff_dev, half_width), BF16),
+        pltpu.VMEM((blocks, rows_dev * heads_dev, head_size), BF16),
+        pltpu.VMEM((rows * heads_dev, head_size), F32),
+        pltpu.VMEM((rows, heads_dev * head_size), BF16),
+        pltpu.VMEM((rows, cols), F32),
+        pltpu.VMEM((rows, cols), F32),
+        pltpu.VMEM((rows, cols), BF16),
+        pltpu.VMEM((half_blocks, rows, cols), BF16),
+        pltpu.VMEM((blocks, 1, 128), F32),
+        pltpu.VMEM((rows, ff_dev), F32),
+        pltpu.VMEM((rows, ff_dev), F32),
+        pltpu.VMEM((rows, ff_dev), F32),
+        pltpu.VMEM((rows, ff_dev), F32),
+        pltpu.VMEM((rows, names), F32),
+        pltpu.VMEM((rows, names), F32),
+        pltpu.VMEM((blocks, rows_dev, half_width), F32),
+        pltpu.VMEM((blocks, rows_dev, half_width), F32),
+        dma((11,)),
+        dma((blocks,)),
+        dma((blocks,)),
+        dma((experts_axis,)),
+        dma((half_blocks,)),
+        dma((blocks,)),
+        dma((blocks,)),
+        dma((4,)),
+        dma((4,)),
+        dma((blocks,)),
+        dma((blocks,)),
+    ]
+    out = pl.pallas_call(
+        functools.partial(step_kernel, experts_axis, dp_axis),
+        out_shape=jax.ShapeDtypeStruct((rows_dev, half_width), F32),
+        in_specs=[pl.BlockSpec(memory_space=pltpu.SMEM), any_spec, vmem_spec, vmem_spec]
+        + [any_spec] * 10,
+        out_specs=vmem_spec,
+        scratch_shapes=scratch,
+        compiler_params=pltpu.CompilerParams(
+            collective_id=0, has_side_effects=True, vmem_limit_bytes=60 * 1024 * 1024
+        ),
+    )(
+        lengths,
+        queries,
+        new_key,
+        new_value,
+        key_cache.reshape(rows_dev, cached, head_size),
+        value_cache.reshape(rows_dev, cached, head_size),
+        w_out,
+        resid_cols,
+        norm_gain[None, :],
+        router,
+        routes,
+        w_gate[0],
+        w_up[0],
+        w_down[0],
+    )
+    return out.astype(BF16)
+
+
 def solution(mesh):
     in_specs = (
         P(("groups", "expert", "dp"), "head", None),
@@ -124,4 +590,6 @@
         P("expert", "dp", "head"),
     )
     out_specs = P(("groups", "expert", "dp"), "head")
-    return jax.shard_map(body, mesh=mesh, in_specs=in_specs, out_specs=out_specs, check_vma=False)
+    return jax.shard_map(
+        functools.partial(body, mesh.shape["expert"], mesh.shape["dp"]),
+        mesh=mesh, in_specs=in_specs, out_specs=out_specs, check_vma=False)

time: 181 us -> 28.7 us (0.16)
  waiting for transfers between devices: 72.4 us -> 0 us
  blocking collectives: 69.8 us -> 0 us
  Pallas kernels: 0 us -> 25.7 us
  between operations: 14.2 us -> 0.01 us
  matrix products: 11.8 us -> 0 us
  starting transfers between devices: 5.5 us -> 0 us
  other arithmetic: 4.9 us -> 1.32 us
    unnamed x2 -> x0, waiting for transfers between devices: 66 us -> none
    all_gather x2 -> x0, blocking collectives: 62.8 us -> none  [the longest x1 32.3 us: body(): lax.all_gather(attn, ('expert', 'dp'), axis=0, tiled=True)]
    pallas_call x0 -> x1, Pallas kernels: none -> 25.7 us  [body(): pl.pallas_call(functools.partial(step_kernel, experts_axis, dp_axis), out...]
    dot_general x9 -> x0, matrix products: 11.8 us -> none  [the longest x1 2.83 us: body(): jnp.dot(lax.all_gather(attn, ('expert', 'dp'), axis=0, tiled=True), w_out...]
    psum x2 -> x0, blocking collectives: 6.96 us -> none  [the longest x1 3.55 us: body(): expert_gate, expert_up = lax.psum((gate_part, up_part), 'head')]
    all_to_all x1 -> x0, waiting for transfers between devices: 6.37 us -> none  [body(): lax.all_to_all(hidden_cols, ('expert', 'dp'), split_axis=0, concat_axis=1...]
    all_to_all x1 -> x0, starting transfers between devices: 5.46 us -> none  [body(): lax.all_to_all(hidden_cols, ('expert', 'dp'), split_axis=0, concat_axis=1...]
  transfers between devices with their start and end apart: 2 -> 0, of which waited for: 2 -> 0; matrix products, arithmetic and copies ran while one was open for 0% -> 0% of each run, Pallas kernels for 0% -> 0%
where the time goes in v1:
time: 28.7 us; the launch traced here: 28.4 us
  Pallas kernels  25.7 us (90%)
  local copies, waits for them, and re-layouts  1.35 us (5%)
  other arithmetic  1.32 us (5%)
    pallas_call x1, Pallas kernels, body(): pl.pallas_call(functools.partial(step_kernel, experts_axis, dp_axis), out...  25.7 us
    unnamed x1, local copies, waits for them, and re-layouts  1.35 us
    convert_element_type x1, other arithmetic, body(): return out.astype(BF16)  1.32 us

profile of v1, /device:TPU:0, one launch (start us, length us, event | category | flops | bytes accessed | tf_op | source)
XLA Modules:
  0.0 28.4 jit_solution(4884870191471213667)
XLA Ops:
  0.0 1.4 %copy.15.routes = s32[16,8]{1,0:T(8,128)} copy(s32[16,8]{0,1:T(8,128)} %param.25) | data formatting | bytes 1024 | tf_op args[10]
  1.4 25.7 %shard_map.136 = f32[2,2048]{1,0:T(2,128)} custom-call(s32[2]{0:T(128)} %lengths.1, bf16[2,32,128]{2,1,0:T(8,128)(2,1)} %queries.1, bf16[2,2,128]{2,1,0:T(2,128)(2,1)} %new_key.1, bf16[2,2,128]{2,1,0:T(2,128)(2,1)} %new_value.1, bf16[2,1024,128]{2,1,0:T(8,128)(2,1)} %bitcast.9, bf16[2,1024,128]{2,1,0:T(8,128)(2,1)} %bitcast.10, bf16[4096,512]{1,0:T(8,128)(2,1)} %w_out.1, ...), custom_call_target="tpu_custom_call" | custom-call | tf_op jit(solution)/shard_map/pallas_call | solution.py:545
  27.0 1.3 %convert_element_type.3 = bf16[2,2048]{1,0:T(2,128)(2,1)} convert(f32[2,2048]{1,0:T(2,128)} %shard_map.136) | non-fusion elementwise | flops 4096 | bytes 24576 | tf_op jit(solution)/shard_map/convert_element_type | solution.py:571

commit v2 on v1

--- a/solution.py
+++ b/solution.py
@@ -132,6 +132,9 @@
     w_down,
     out,
     q_v,
+    lengths_v,
+    nk_v,
+    nv_v,
     k_v,
     v_v,
     wo_v,
@@ -149,13 +152,15 @@
     proj_other,
     hid_send,
     hid_all,
-    sq_all,
+    sq_mine,
+    sq_other,
     gate_mine,
     gate_other,
     up_mine,
     up_other,
     logit_mine,
     logit_other,
+    y_mine,
     y_send,
     y_recv,
     load_sem,
@@ -163,8 +168,6 @@
     attn_rsem,
     hid_ssem,
     hid_rsem,
-    sq_ssem,
-    sq_rsem,
     pair_ssem,
     pair_rsem,
     y_ssem,
@@ -189,21 +192,23 @@
         }
 
     def peer(k):
-        return lax.rem(me + k, blocks)
-
-    barrier = pltpu.get_barrier_semaphore()
-    for k in range(blocks):
-        if k:
-            pl.semaphore_signal(barrier, 1, device_id=device(peer(k), head), device_id_type=MESH)
-        pl.semaphore_signal(barrier, 1, device_id=device(peer(k), 1 - head), device_id_type=MESH)
+        other, rest, bit = 0, me, 1
+        while bit < blocks:
+            digit = lax.rem(rest, 2)
+            other = other + bit * (1 - digit if k & bit else digit)
+            rest, bit = lax.div(rest, 2), 2 * bit
+        return other
 
     half_start = pl.multiple_of(head * half_width, half_width)
     loads = [
         pltpu.make_async_copy(src, dst, load_sem.at[i])
         for i, (src, dst) in enumerate(
             (
+                (keys, k_v),
                 (queries, q_v),
-                (keys, k_v),
+                (lengths, lengths_v),
+                (new_key, nk_v),
+                (new_value, nv_v),
                 (values, v_v),
                 (w_out, wo_v),
                 (resid, res_v),
@@ -216,9 +221,15 @@
             )
         )
     ]
-    for load in loads:
+    for load in loads[:6]:
         load.start()
-    (ld_q, ld_k, ld_v, ld_wo, ld_res, ld_gain, ld_routes, ld_rt, ld_wg, ld_wu, ld_wd) = loads
+
+    barrier = pltpu.get_barrier_semaphore()
+    for k in reversed(range(blocks)):
+        if k:
+            pl.semaphore_signal(barrier, 1, device_id=device(peer(k), head), device_id_type=MESH)
+        pl.semaphore_signal(barrier, 1, device_id=device(peer(k), 1 - head), device_id_type=MESH)
+    (ld_k, ld_q, ld_len, ld_nk, ld_nv, ld_v, ld_wo, ld_res, ld_gain, ld_routes, ld_rt, ld_wg, ld_wu, ld_wd) = loads
 
     cached = keys.shape[1]
     scale = head_size ** (-0.5)
@@ -228,8 +239,13 @@
     same_kv = lax.rem(column, kv_dev) == lax.div(head_of, group_size)
     kv_of = lax.div(lax.broadcasted_iota(jnp.int32, (heads_dev, head_size), 0), group_size)
     ld_q.wait()
+    ld_len.wait()
+    ld_nk.wait()
+    ld_nv.wait()
     ld_k.wait()
     ld_v.wait()
+    for load in loads[6:]:
+        load.start()
     for r in range(rows_dev):
         q = q_v[r]
         scores = (
@@ -239,10 +255,10 @@
         fresh_key = jnp.zeros((heads_dev, head_size), F32)
         fresh_value = jnp.zeros((heads_dev, head_size), F32)
         for k in range(kv_dev):
-            fresh_key = jnp.where(kv_of == k, new_key[r, k : k + 1, :].astype(F32), fresh_key)
-            fresh_value = jnp.where(kv_of == k, new_value[r, k : k + 1, :].astype(F32), fresh_value)
+            fresh_key = jnp.where(kv_of == k, nk_v[r, k : k + 1, :].astype(F32), fresh_key)
+            fresh_value = jnp.where(kv_of == k, nv_v[r, k : k + 1, :].astype(F32), fresh_value)
         score_new = jnp.sum(q.astype(F32) * fresh_key, axis=-1, keepdims=True) * scale
-        scores = jnp.where(same_kv & (position < lengths[r]), scores, -jnp.inf)
+        scores = jnp.where(same_kv & (position < lengths_v[r]), scores, -jnp.inf)
         highest = jnp.maximum(jnp.max(scores, axis=-1, keepdims=True), score_new)
         exp_cache = jnp.exp(scores - highest)
         exp_new = jnp.exp(score_new - highest)
@@ -285,7 +301,7 @@
             device_id_type=MESH,
         )
 
-    sends = [exchange(attn_all, attn_ssem, attn_rsem, k) for k in range(1, blocks)]
+    sends = [exchange(attn_all, attn_ssem, attn_rsem, k) for k in reversed(range(1, blocks))]
     for copy in sends:
         copy.start()
     block_rows = rows_dev * heads_dev
@@ -297,16 +313,24 @@
     widen(me)
 
     ld_routes.wait()
-    picks = routes_v[...]
     expert_ids = lax.broadcasted_iota(jnp.int32, (rows, router.shape[1]), 1)
-    picked = expert_ids == picks[:, 0:1]
-    for k in range(1, picks.shape[1]):
-        picked = picked | (expert_ids == picks[:, k : k + 1])
-    own = jnp.min(picks, axis=1, keepdims=True)
+    row_is_lane = lax.broadcasted_iota(jnp.int32, (rows, rows), 0) == lax.broadcasted_iota(
+        jnp.int32, (rows, rows), 1
+    )
+
+    def pick(k):
+        return jnp.sum(jnp.where(row_is_lane, routes_v[k : k + 1, :], 0), axis=1, keepdims=True)
+
+    own = pick(0)
+    picked = expert_ids == own
+    for k in range(1, routes.shape[0]):
+        chosen = pick(k)
+        picked = picked | (expert_ids == chosen)
+        own = jnp.minimum(own, chosen)
     is_mine = own == expert
 
     for k in range(1, blocks):
-        block = peer(blocks - k)
+        block = peer(k)
         arrival(attn_all.at[block], attn_all.at[block], attn_ssem, attn_rsem, block).wait_recv()
         widen(block)
     for h in range(heads_dev):
@@ -323,18 +347,13 @@
     proj_copy.wait_recv()
     hidden = (res_v[...].astype(F32) + (proj_mine[...] + proj_other[...])).astype(BF16)
     hid_send[...] = hidden
-    squares = hidden.astype(F32)
-    squares = jnp.sum(squares * squares, axis=-1, keepdims=True)
-    row_is_lane = lax.broadcasted_iota(jnp.int32, (rows, 128), 0) == lax.broadcasted_iota(
-        jnp.int32, (rows, 128), 1
-    )
     half_of = lax.div(me, half_blocks)
     slot = lax.rem(me, half_blocks)
     stays = head == half_of
     target_dp = lax.rem(dp + jnp.where(stays, 0, 1), dp_axis)
 
     def hid_copy(k):
-        to = lax.rem(expert + k, experts_axis)
+        to = lax.div(peer(k * dp_axis), dp_axis)
         return pltpu.make_async_remote_copy(
             src_ref=hid_send,
             dst_ref=hid_all.at[slot],
@@ -344,7 +363,7 @@
             device_id_type=MESH,
         )
 
-    for k in range(1, experts_axis):
+    for k in reversed(range(1, experts_axis)):
         hid_copy(k).start()
 
     @pl.when(jnp.logical_not(stays))
@@ -355,17 +374,9 @@
     def _():
         hid_all[slot] = hidden
 
-    sq_all[me] = jnp.sum(jnp.where(row_is_lane, squares, 0.0), axis=0, keepdims=True)
-    sq_sends = [exchange(sq_all, sq_ssem, sq_rsem, k) for k in range(1, blocks)]
-    for copy in sq_sends:
-        copy.start()
-    total = sq_all[me]
-    for k in range(1, blocks):
-        block = peer(blocks - k)
-        arrival(sq_all.at[block], sq_all.at[block], sq_ssem, sq_rsem, block).wait_recv()
-        total = total + sq_all[block]
-    total = jnp.sum(jnp.where(row_is_lane, total, 0.0), axis=1, keepdims=True)
-    inverse_rms = lax.rsqrt(total / (2 * half_width) + 1e-06)
+    for copy in sends + [proj_copy]:
+        copy.wait_send()
+
     for i in range(half_blocks):
 
         @pl.when(jnp.logical_not(stays & (slot == i)))
@@ -379,16 +390,29 @@
                 device_id_type=MESH,
             ).wait_recv()
 
+    lanes = sq_mine.shape[1]
+    squares = jnp.zeros(sq_mine.shape, F32)
+    blocks_f32 = [hid_all[i].astype(F32) for i in range(half_blocks)]
+    for block in blocks_f32:
+        for start in range(0, cols, lanes):
+            part = block[:, start : start + lanes]
+            squares = squares + part * part
+    sq_mine[...] = squares
+    sq_copy = to_sibling(sq_mine, sq_other, 4)
+    sq_copy.start()
     row_index = lax.broadcasted_iota(jnp.int32, (rows, 1), 0)
     is_own_row = lax.div(row_index, rows_dev) == me
-    kept, pieces = [], []
-    for i in range(half_blocks):
-        values_f32 = hid_all[i].astype(F32)
-        kept.append(jnp.where(is_own_row, values_f32, 0.0))
-        pieces.append(
-            (values_f32 * inverse_rms * gain_v[:, i * cols : (i + 1) * cols]).astype(BF16)
-        )
-    normed = jnp.concatenate(pieces, axis=1)
+    kept = [jnp.where(is_own_row, block, 0.0) for block in blocks_f32]
+    sq_copy.wait_recv()
+    total = jnp.sum(sq_mine[...] + sq_other[...], axis=1, keepdims=True)
+    inverse_rms = lax.rsqrt(total / (2 * half_width) + 1e-06)
+    normed = jnp.concatenate(
+        [
+            (block * inverse_rms * gain_v[:, i * cols : (i + 1) * cols]).astype(BF16)
+            for i, block in enumerate(blocks_f32)
+        ],
+        axis=1,
+    )
 
     ld_wg.wait()
     gate_mine[...] = jnp.dot(normed, wg_v[...], preferred_element_type=F32)
@@ -403,6 +427,14 @@
     up_copy = to_sibling(up_mine, up_other, 3)
     up_copy.start()
 
+    sq_copy.wait_send()
+    for k in range(1, experts_axis):
+        hid_copy(k).wait_send()
+
+    @pl.when(jnp.logical_not(stays))
+    def _():
+        hid_copy(0).wait_send()
+
     logit_copy.wait_recv()
     logits = jnp.where(picked, logit_mine[...] + logit_other[...], -jnp.inf)
     weights = jnp.exp(logits - jnp.max(logits, axis=1, keepdims=True))
@@ -418,11 +450,16 @@
     activated = (gate * (up_mine[...] + up_other[...])).astype(BF16)
     routed = jnp.dot(activated, wd_v[...], preferred_element_type=F32) * row_share
     routed = routed + jnp.concatenate(kept, axis=1)
+    piece = y_mine.shape[2]
     for block in range(blocks):
-        y_send[block] = routed[block * rows_dev : (block + 1) * rows_dev, :]
+        for i in range(half_width // piece):
+            y_mine[block, i * rows_dev : (i + 1) * rows_dev, :] = routed[
+                block * rows_dev : (block + 1) * rows_dev, i * piece : (i + 1) * piece
+            ]
+        y_send[block] = y_mine[block].astype(BF16)
 
     y_sends = []
-    for k in range(1, blocks):
+    for k in reversed(range(1, blocks)):
         to = peer(k)
         y_sends.append(
             pltpu.make_async_remote_copy(
@@ -436,21 +473,15 @@
         )
     for copy in y_sends:
         copy.start()
-    result = y_send[me]
+    for copy in [gate_copy, logit_copy, up_copy] + y_sends:
+        copy.wait_send()
+    result = y_mine[me]
     for k in range(1, blocks):
-        block = peer(blocks - k)
+        block = peer(k)
         arrival(y_send.at[block], y_recv.at[block], y_ssem, y_rsem, block).wait_recv()
-        result = result + y_recv[block]
-    out[...] = result
-
-    for copy in sends + sq_sends + y_sends + [proj_copy, gate_copy, logit_copy, up_copy]:
-        copy.wait_send()
-    for k in range(1, experts_axis):
-        hid_copy(k).wait_send()
-
-    @pl.when(jnp.logical_not(stays))
-    def _():
-        hid_copy(0).wait_send()
+        result = result + y_recv[block].astype(F32)
+    for i in range(half_width // piece):
+        out[:, i * piece : (i + 1) * piece] = result[i * rows_dev : (i + 1) * rows_dev, :]
 
 
 def body(
@@ -479,7 +510,7 @@
     cols = w_out.shape[1]
     half_width, ff_dev = w_gate.shape[1:]
     names = router.shape[1]
-    if cols % 128 or ff_dev % 128 or rows > 64 or rows % 16 or blocks % 2 or dp_axis != 2:
+    if cols % 128 or ff_dev % 128 or rows > 64 or rows % 16 or blocks & (blocks - 1) or dp_axis != 2 or rows_dev != 2:
         return plain_body(
             queries,
             new_key,
@@ -498,19 +529,22 @@
             w_down,
         )
     half_blocks = blocks // 2
+    tile = 16
     dma = pltpu.SemaphoreType.DMA
-    any_spec = pl.BlockSpec(memory_space=pl.ANY)
     vmem_spec = pl.BlockSpec(memory_space=pltpu.VMEM)
     cached = cache_len * kv_dev
     scratch = [
         pltpu.VMEM((rows_dev, heads_dev, head_size), BF16),
+        pltpu.SMEM((rows_dev,), jnp.int32),
+        pltpu.VMEM(new_key.shape, BF16),
+        pltpu.VMEM(new_value.shape, BF16),
         pltpu.VMEM((rows_dev, cached, head_size), BF16),
         pltpu.VMEM((rows_dev, cached, head_size), BF16),
         pltpu.VMEM(w_out.shape, BF16),
         pltpu.VMEM(resid_cols.shape, BF16),
         pltpu.VMEM((1, half_width), F32),
         pltpu.VMEM((half_width, names), BF16),
-        pltpu.VMEM(routes.shape, jnp.int32),
+        pltpu.VMEM(routes.shape[::-1], jnp.int32),
         pltpu.VMEM((half_width, ff_dev), BF16),
         pltpu.VMEM((half_width, ff_dev), BF16),
         pltpu.VMEM((ff_dev, half_width), BF16),
@@ -521,32 +555,31 @@
         pltpu.VMEM((rows, cols), F32),
         pltpu.VMEM((rows, cols), BF16),
         pltpu.VMEM((half_blocks, rows, cols), BF16),
-        pltpu.VMEM((blocks, 1, 128), F32),
+        pltpu.VMEM((rows, 128), F32),
+        pltpu.VMEM((rows, 128), F32),
         pltpu.VMEM((rows, ff_dev), F32),
         pltpu.VMEM((rows, ff_dev), F32),
         pltpu.VMEM((rows, ff_dev), F32),
         pltpu.VMEM((rows, ff_dev), F32),
         pltpu.VMEM((rows, names), F32),
         pltpu.VMEM((rows, names), F32),
-        pltpu.VMEM((blocks, rows_dev, half_width), F32),
-        pltpu.VMEM((blocks, rows_dev, half_width), F32),
-        dma((11,)),
+        pltpu.VMEM((blocks, tile, rows_dev * half_width // tile), F32),
+        pltpu.VMEM((blocks, tile, rows_dev * half_width // tile), BF16),
+        pltpu.VMEM((blocks, tile, rows_dev * half_width // tile), BF16),
+        dma((14,)),
         dma((blocks,)),
         dma((blocks,)),
         dma((experts_axis,)),
         dma((half_blocks,)),
-        dma((blocks,)),
-        dma((blocks,)),
-        dma((4,)),
-        dma((4,)),
+        dma((5,)),
+        dma((5,)),
         dma((blocks,)),
         dma((blocks,)),
     ]
     out = pl.pallas_call(
         functools.partial(step_kernel, experts_axis, dp_axis),
-        out_shape=jax.ShapeDtypeStruct((rows_dev, half_width), F32),
-        in_specs=[pl.BlockSpec(memory_space=pltpu.SMEM), any_spec, vmem_spec, vmem_spec]
-        + [any_spec] * 10,
+        out_shape=pltpu.VMEM((rows_dev, half_width), F32),
+        in_specs=[pl.BlockSpec(memory_space=pl.ANY)] * 14,
         out_specs=vmem_spec,
         scratch_shapes=scratch,
         compiler_params=pltpu.CompilerParams(
@@ -563,7 +596,7 @@
         resid_cols,
         norm_gain[None, :],
         router,
-        routes,
+        routes.T,
         w_gate[0],
         w_up[0],
         w_down[0],

time: 28.7 us -> 25.8 us (0.90)
  local copies, waits for them, and re-layouts: 1.35 us -> 0 us
  other arithmetic: 1.32 us -> 0.61 us
  Pallas kernels: 25.7 us -> 25 us
    unnamed x1 -> x0, local copies, waits for them, and re-layouts: 1.35 us -> none
    convert_element_type x1, other arithmetic: 1.32 us -> 0.61 us  [body(): return out.astype(BF16)]
    pallas_call x1, Pallas kernels: 25.7 us -> 25 us  [body(): pl.pallas_call(functools.partial(step_kernel, experts_axis, dp_axis), out...]
where the time goes in v2:
time: 25.8 us; the launch traced here: 25.6 us
  Pallas kernels  25 us (97%)
  other arithmetic  0.61 us (2%)
    pallas_call x1, Pallas kernels, body(): pl.pallas_call(functools.partial(step_kernel, experts_axis, dp_axis), out...  25 us
    convert_element_type x1, other arithmetic, body(): return out.astype(BF16)  0.61 us

profile of v2, /device:TPU:0, one launch (start us, length us, event | category | flops | bytes accessed | tf_op | source)
XLA Modules:
  0.0 25.6 jit_solution(10572539683192728574)
XLA Ops:
  0.0 25.0 %shard_map.136 = f32[2,2048]{1,0:T(2,128)S(1)} custom-call(s32[2]{0:T(128)} %lengths.1, bf16[2,32,128]{2,1,0:T(8,128)(2,1)} %queries.1, bf16[2,2,128]{2,1,0:T(2,128)(2,1)} %new_key.1, bf16[2,2,128]{2,1,0:T(2,128)(2,1)} %new_value.1, bf16[2,1024,128]{2,1,0:T(8,128)(2,1)} %bitcast.10, bf16[2,1024,128]{2,1,0:T(8,128)(2,1)} %bitcast.11, ...), custom_call_target="tpu_custom_call" | custom-call | tf_op jit(solution)/shard_map/pallas_call | solution.py:579
  25.0 0.6 %convert_element_type.3 = bf16[2,2048]{1,0:T(2,128)(2,1)} convert(f32[2,2048]{1,0:T(2,128)S(1)} %shard_map.136) | non-fusion elementwise | flops 4096 | bytes 24576 | tf_op jit(solution)/shard_map/convert_element_type | solution.py:604

commit v3 on v2

--- a/solution.py
+++ b/solution.py
@@ -153,7 +153,7 @@
     hid_send,
     hid_all,
     sq_mine,
-    sq_other,
+    sq_all,
     gate_mine,
     gate_other,
     up_mine,
@@ -168,6 +168,8 @@
     attn_rsem,
     hid_ssem,
     hid_rsem,
+    sq_ssem,
+    sq_rsem,
     pair_ssem,
     pair_rsem,
     y_ssem,
@@ -198,6 +200,12 @@
             other = other + bit * (1 - digit if k & bit else digit)
             rest, bit = lax.div(rest, 2), 2 * bit
         return other
+
+    barrier = pltpu.get_barrier_semaphore()
+    for k in reversed(range(blocks)):
+        if k:
+            pl.semaphore_signal(barrier, 1, device_id=device(peer(k), head), device_id_type=MESH)
+        pl.semaphore_signal(barrier, 1, device_id=device(peer(k), 1 - head), device_id_type=MESH)
 
     half_start = pl.multiple_of(head * half_width, half_width)
     loads = [
@@ -223,12 +231,6 @@
     ]
     for load in loads[:6]:
         load.start()
-
-    barrier = pltpu.get_barrier_semaphore()
-    for k in reversed(range(blocks)):
-        if k:
-            pl.semaphore_signal(barrier, 1, device_id=device(peer(k), head), device_id_type=MESH)
-        pl.semaphore_signal(barrier, 1, device_id=device(peer(k), 1 - head), device_id_type=MESH)
     (ld_k, ld_q, ld_len, ld_nk, ld_nv, ld_v, ld_wo, ld_res, ld_gain, ld_routes, ld_rt, ld_wg, ld_wu, ld_wd) = loads
 
     cached = keys.shape[1]
@@ -243,30 +245,43 @@
     ld_nk.wait()
     ld_nv.wait()
     ld_k.wait()
-    ld_v.wait()
     for load in loads[6:]:
         load.start()
-    for r in range(rows_dev):
-        q = q_v[r]
-        scores = (
-            lax.dot_general(q, k_v[r], (((1,), (1,)), ((), ())), preferred_element_type=F32)
-            * scale
-        )
+    each = range(rows_dev)
+    scores = [
+        lax.dot_general(q_v[r], k_v[r], (((1,), (1,)), ((), ())), preferred_element_type=F32)
+        for r in each
+    ]
+    fresh_keys, fresh_values = [], []
+    for r in each:
         fresh_key = jnp.zeros((heads_dev, head_size), F32)
         fresh_value = jnp.zeros((heads_dev, head_size), F32)
         for k in range(kv_dev):
             fresh_key = jnp.where(kv_of == k, nk_v[r, k : k + 1, :].astype(F32), fresh_key)
             fresh_value = jnp.where(kv_of == k, nv_v[r, k : k + 1, :].astype(F32), fresh_value)
-        score_new = jnp.sum(q.astype(F32) * fresh_key, axis=-1, keepdims=True) * scale
-        scores = jnp.where(same_kv & (position < lengths_v[r]), scores, -jnp.inf)
-        highest = jnp.maximum(jnp.max(scores, axis=-1, keepdims=True), score_new)
-        exp_cache = jnp.exp(scores - highest)
-        exp_new = jnp.exp(score_new - highest)
-        inverse = 1.0 / (jnp.sum(exp_cache, axis=-1, keepdims=True) + exp_new)
-        probs = (exp_cache * inverse).astype(BF16)
-        probs_new = (exp_new * inverse).astype(BF16).astype(F32)
-        mixed = jnp.dot(probs, v_v[r], preferred_element_type=F32) + probs_new * fresh_value
-        attn_all[me, r * heads_dev : (r + 1) * heads_dev, :] = mixed.astype(BF16)
+        fresh_keys.append(fresh_key)
+        fresh_values.append(fresh_value)
+    score_new = [
+        jnp.sum(q_v[r].astype(F32) * fresh_keys[r], axis=-1, keepdims=True) * scale for r in each
+    ]
+    scores = [
+        jnp.where(same_kv & (position < lengths_v[r]), scores[r] * scale, -jnp.inf) for r in each
+    ]
+    highest = [
+        jnp.maximum(jnp.max(scores[r], axis=-1, keepdims=True), score_new[r]) for r in each
+    ]
+    exp_cache = [jnp.exp(scores[r] - highest[r]) for r in each]
+    exp_new = [jnp.exp(score_new[r] - highest[r]) for r in each]
+    inverse = [
+        1.0 / (jnp.sum(exp_cache[r], axis=-1, keepdims=True) + exp_new[r]) for r in each
+    ]
+    probs = [(exp_cache[r] * inverse[r]).astype(BF16) for r in each]
+    probs_new = [(exp_new[r] * inverse[r]).astype(BF16).astype(F32) for r in each]
+    ld_v.wait()
+    mixed = [jnp.dot(probs[r], v_v[r], preferred_element_type=F32) for r in each]
+    for r in each:
+        attn = mixed[r] + probs_new[r] * fresh_values[r]
+        attn_all[me, r * heads_dev : (r + 1) * heads_dev, :] = attn.astype(BF16)
 
     pl.semaphore_wait(barrier, 2 * blocks - 1)
 
@@ -363,6 +378,25 @@
             device_id_type=MESH,
         )
 
+    sq_dp = lax.rem(dp + jnp.where(stays, 1, 0), dp_axis)
+
+    def sq_copy(k):
+        to = lax.div(peer(k * dp_axis), dp_axis)
+        return pltpu.make_async_remote_copy(
+            src_ref=sq_mine,
+            dst_ref=sq_all.at[slot],
+            send_sem=sq_ssem.at[k],
+            recv_sem=sq_rsem.at[slot],
+            device_id={"expert": to, "dp": sq_dp, "head": 1 - half_of},
+            device_id_type=MESH,
+        )
+
+    def lane_squares(block, total):
+        for start in range(0, cols, total.shape[1]):
+            part = block[:, start : start + total.shape[1]]
+            total = total + part * part
+        return total
+
     for k in reversed(range(1, experts_axis)):
         hid_copy(k).start()
 
@@ -370,9 +404,19 @@
     def _():
         hid_copy(0).start()
 
+    own_squares = lane_squares(hidden.astype(F32), jnp.zeros(sq_mine.shape, F32))
+    sq_mine[...] = own_squares
+    for k in reversed(range(1, experts_axis)):
+        sq_copy(k).start()
+
     @pl.when(stays)
     def _():
+        sq_copy(0).start()
         hid_all[slot] = hidden
+
+    @pl.when(jnp.logical_not(stays))
+    def _():
+        sq_all[slot] = own_squares
 
     for copy in sends + [proj_copy]:
         copy.wait_send()
@@ -390,21 +434,28 @@
                 device_id_type=MESH,
             ).wait_recv()
 
-    lanes = sq_mine.shape[1]
     squares = jnp.zeros(sq_mine.shape, F32)
     blocks_f32 = [hid_all[i].astype(F32) for i in range(half_blocks)]
     for block in blocks_f32:
-        for start in range(0, cols, lanes):
-            part = block[:, start : start + lanes]
-            squares = squares + part * part
-    sq_mine[...] = squares
-    sq_copy = to_sibling(sq_mine, sq_other, 4)
-    sq_copy.start()
+        squares = lane_squares(block, squares)
+    for i in range(half_blocks):
+
+        @pl.when(stays | (slot != i))
+        def _():
+            pltpu.make_async_remote_copy(
+                src_ref=sq_mine,
+                dst_ref=sq_all.at[i],
+                send_sem=sq_ssem.at[0],
+                recv_sem=sq_rsem.at[i],
+                device_id=device(me, 1 - head),
+                device_id_type=MESH,
+            ).wait_recv()
+
+        squares = squares + sq_all[i]
     row_index = lax.broadcasted_iota(jnp.int32, (rows, 1), 0)
     is_own_row = lax.div(row_index, rows_dev) == me
     kept = [jnp.where(is_own_row, block, 0.0) for block in blocks_f32]
-    sq_copy.wait_recv()
-    total = jnp.sum(sq_mine[...] + sq_other[...], axis=1, keepdims=True)
+    total = jnp.sum(squares, axis=1, keepdims=True)
     inverse_rms = lax.rsqrt(total / (2 * half_width) + 1e-06)
     normed = jnp.concatenate(
         [
@@ -427,9 +478,13 @@
     up_copy = to_sibling(up_mine, up_other, 3)
     up_copy.start()
 
-    sq_copy.wait_send()
     for k in range(1, experts_axis):
         hid_copy(k).wait_send()
+        sq_copy(k).wait_send()
+
+    @pl.when(stays)
+    def _():
+        sq_copy(0).wait_send()
 
     @pl.when(jnp.logical_not(stays))
     def _():
@@ -473,8 +528,6 @@
         )
     for copy in y_sends:
         copy.start()
-    for copy in [gate_copy, logit_copy, up_copy] + y_sends:
-        copy.wait_send()
     result = y_mine[me]
     for k in range(1, blocks):
         block = peer(k)
@@ -482,6 +535,8 @@
         result = result + y_recv[block].astype(F32)
     for i in range(half_width // piece):
         out[:, i * piece : (i + 1) * piece] = result[i * rows_dev : (i + 1) * rows_dev, :]
+    for copy in [gate_copy, logit_copy, up_copy] + y_sends:
+        copy.wait_send()
 
 
 def body(
@@ -556,7 +611,7 @@
         pltpu.VMEM((rows, cols), BF16),
         pltpu.VMEM((half_blocks, rows, cols), BF16),
         pltpu.VMEM((rows, 128), F32),
-        pltpu.VMEM((rows, 128), F32),
+        pltpu.VMEM((half_blocks, rows, 128), F32),
         pltpu.VMEM((rows, ff_dev), F32),
         pltpu.VMEM((rows, ff_dev), F32),
         pltpu.VMEM((rows, ff_dev), F32),
@@ -571,8 +626,10 @@
         dma((blocks,)),
         dma((experts_axis,)),
         dma((half_blocks,)),
-        dma((5,)),
-        dma((5,)),
+        dma((experts_axis,)),
+        dma((half_blocks,)),
+        dma((4,)),
+        dma((4,)),
         dma((blocks,)),
         dma((blocks,)),
     ]

time: 25.8 us -> 25.2 us (0.977)
  Pallas kernels: 25 us -> 24.5 us
    pallas_call x1, Pallas kernels: 25 us -> 24.5 us  [body(): pl.pallas_call(functools.partial(step_kernel, experts_axis, dp_axis), out...]
where the time goes in v3:
time: 25.2 us; the launch traced here: 25.1 us
  Pallas kernels  24.5 us (97%)
  other arithmetic  0.61 us (2%)
    pallas_call x1, Pallas kernels, body(): pl.pallas_call(functools.partial(step_kernel, experts_axis, dp_axis), out...  24.5 us
    convert_element_type x1, other arithmetic, body(): return out.astype(BF16)  0.61 us

profile of v3, /device:TPU:0, one launch (start us, length us, event | category | flops | bytes accessed | tf_op | source)
XLA Modules:
  0.0 25.1 jit_solution(7629601338054815325)
XLA Ops:
  0.0 24.5 %shard_map.136 = f32[2,2048]{1,0:T(2,128)S(1)} custom-call(s32[2]{0:T(128)} %lengths.1, bf16[2,32,128]{2,1,0:T(8,128)(2,1)} %queries.1, bf16[2,2,128]{2,1,0:T(2,128)(2,1)} %new_key.1, bf16[2,2,128]{2,1,0:T(2,128)(2,1)} %new_value.1, bf16[2,1024,128]{2,1,0:T(8,128)(2,1)} %bitcast.10, bf16[2,1024,128]{2,1,0:T(8,128)(2,1)} %bitcast.11, ...), custom_call_target="tpu_custom_call" | custom-call | tf_op jit(solution)/shard_map/pallas_call | solution.py:636
  24.5 0.6 %convert_element_type.3 = bf16[2,2048]{1,0:T(2,128)(2,1)} convert(f32[2,2048]{1,0:T(2,128)S(1)} %shard_map.136) | non-fusion elementwise | flops 4096 | bytes 24576 | tf_op jit(solution)/shard_map/convert_element_type | solution.py:661

commit v4 on v3

--- a/solution.py
+++ b/solution.py
@@ -277,21 +277,15 @@
     ]
     probs = [(exp_cache[r] * inverse[r]).astype(BF16) for r in each]
     probs_new = [(exp_new[r] * inverse[r]).astype(BF16).astype(F32) for r in each]
-    ld_v.wait()
-    mixed = [jnp.dot(probs[r], v_v[r], preferred_element_type=F32) for r in each]
-    for r in each:
-        attn = mixed[r] + probs_new[r] * fresh_values[r]
-        attn_all[me, r * heads_dev : (r + 1) * heads_dev, :] = attn.astype(BF16)
-
     pl.semaphore_wait(barrier, 2 * blocks - 1)
 
-    def exchange(buffer, ssem, rsem, k):
+    def exchange(r, k):
         to = peer(k)
         return pltpu.make_async_remote_copy(
-            src_ref=buffer.at[me],
-            dst_ref=buffer.at[me],
-            send_sem=ssem.at[to],
-            recv_sem=rsem.at[me],
+            src_ref=attn_all.at[me, pl.ds(r * heads_dev, heads_dev)],
+            dst_ref=attn_all.at[me, pl.ds(r * heads_dev, heads_dev)],
+            send_sem=attn_ssem.at[r * blocks + to],
+            recv_sem=attn_rsem.at[r * blocks + me],
             device_id=device(to, head),
             device_id_type=MESH,
         )
@@ -302,7 +296,7 @@
             dst_ref=dst,
             send_sem=ssem.at[block],
             recv_sem=rsem.at[block],
-            device_id=device(block, head),
+            device_id=device(lax.rem(block, blocks), head),
             device_id_type=MESH,
         )
 
@@ -316,9 +310,16 @@
             device_id_type=MESH,
         )
 
-    sends = [exchange(attn_all, attn_ssem, attn_rsem, k) for k in reversed(range(1, blocks))]
-    for copy in sends:
-        copy.start()
+    ld_v.wait()
+    sends = []
+    for r in each:
+        mixed = jnp.dot(probs[r], v_v[r], preferred_element_type=F32)
+        attn = mixed + probs_new[r] * fresh_values[r]
+        attn_all[me, r * heads_dev : (r + 1) * heads_dev, :] = attn.astype(BF16)
+        row_sends = [exchange(r, k) for k in reversed(range(1, blocks))]
+        for copy in row_sends:
+            copy.start()
+        sends += row_sends
     block_rows = rows_dev * heads_dev
 
     def widen(block):
@@ -346,7 +347,9 @@
 
     for k in range(1, blocks):
         block = peer(k)
-        arrival(attn_all.at[block], attn_all.at[block], attn_ssem, attn_rsem, block).wait_recv()
+        for r in each:
+            row = attn_all.at[block, pl.ds(r * heads_dev, heads_dev)]
+            arrival(row, row, attn_ssem, attn_rsem, r * blocks + block).wait_recv()
         widen(block)
     for h in range(heads_dev):
         attn_mat[:, h * head_size : (h + 1) * head_size] = attn_f32[
@@ -622,8 +625,8 @@
         pltpu.VMEM((blocks, tile, rows_dev * half_width // tile), BF16),
         pltpu.VMEM((blocks, tile, rows_dev * half_width // tile), BF16),
         dma((14,)),
-        dma((blocks,)),
-        dma((blocks,)),
+        dma((rows_dev * blocks,)),
+        dma((rows_dev * blocks,)),
         dma((experts_axis,)),
         dma((half_blocks,)),
         dma((experts_axis,)),

time: 25.2 us -> 25.5 us (1.012)
    pallas_call x1, Pallas kernels: 24.5 us -> 24.7 us  [body(): pl.pallas_call(functools.partial(step_kernel, experts_axis, dp_axis), out...]
where the time goes in v4:
time: 25.5 us; the launch traced here: 25.4 us
  Pallas kernels  24.7 us (97%)
  other arithmetic  0.61 us (2%)
    pallas_call x1, Pallas kernels, body(): pl.pallas_call(functools.partial(step_kernel, experts_axis, dp_axis), out...  24.7 us
    convert_element_type x1, other arithmetic, body(): return out.astype(BF16)  0.61 us

profile of v4, /device:TPU:0, one launch (start us, length us, event | category | flops | bytes accessed | tf_op | source)
XLA Modules:
  0.0 25.4 jit_solution(8033245311157471748)
XLA Ops:
  0.0 24.7 %shard_map.136 = f32[2,2048]{1,0:T(2,128)S(1)} custom-call(s32[2]{0:T(128)} %lengths.1, bf16[2,32,128]{2,1,0:T(8,128)(2,1)} %queries.1, bf16[2,2,128]{2,1,0:T(2,128)(2,1)} %new_key.1, bf16[2,2,128]{2,1,0:T(2,128)(2,1)} %new_value.1, bf16[2,1024,128]{2,1,0:T(8,128)(2,1)} %bitcast.10, bf16[2,1024,128]{2,1,0:T(8,128)(2,1)} %bitcast.11, ...), custom_call_target="tpu_custom_call" | custom-call | tf_op jit(solution)/shard_map/pallas_call | solution.py:639
  24.8 0.6 %convert_element_type.3 = bf16[2,2048]{1,0:T(2,128)(2,1)} convert(f32[2,2048]{1,0:T(2,128)S(1)} %shard_map.136) | non-fusion elementwise | flops 4096 | bytes 24576 | tf_op jit(solution)/shard_map/convert_element_type | solution.py:664
